TPU v7x, 256 devices: a whole 4x4x8 slice. The times are simulated.
256 devices in a mesh: tm: 32 (over z_hi, y, x), head: 8 (over z_lo, core).
Axes of the slice: x: 4, y: 4, z: 8 (z_hi: 2, z_lo: 4; z = z_hi * 4 + z_lo), core: 2. Of those that a mesh axis runs over, the one named last changes fastest.
Arguments:
- patches: bfloat16 [384, 256, 1152], P('tm', None, 'head'), may hold values from -6 to 6
- grid_rows: int32 [384], P('tm'), may hold values from 8 to 16
- frame_ids: int32 [384], P('tm'), may hold values from 0 to 383, as said below
- ln_gain: float32 [1152], replicated, may hold values from 0.1 to 1.9
- w_qkv: bfloat16 [3, 1152, 1152], P(None, None, 'head'), may hold values from -5.9514821 to 5.9514821
- w_out: bfloat16 [1152, 1152], P('head'), may hold values from -0.1875 to 0.1875
- w_conn: bfloat16 [1152, 4096], P(None, 'head'), may hold values from -0.1875 to 0.1875
- norm_gain: float32 [4096], replicated, may hold values from 0.1 to 1.9
- w_x: bfloat16 [4096, 4096], P(None, 'head'), may hold values from -0.09375 to 0.09375
- w_b: bfloat16 [4096, 1024], P(None, 'head'), may hold values from -0.09375 to 0.09375
- w_c: bfloat16 [4096, 1024], P(None, 'head'), may hold values from -0.09375 to 0.09375
- w_dt: bfloat16 [4096, 64], P(None, 'head'), may hold values from -0.09375 to 0.09375
- dt_bias: float32 [64], P('head'), may hold values from -1 to 1
- a_log: float32 [64], P('head'), may hold values from -14 to -3.2
- d_skip: float32 [64], P('head'), may hold values from 0.5 to 1.5
- out_gain: float32 [4096], P('head'), may hold values from 0.1 to 1.9
Outputs:
- stream: bfloat16 [24576, 4096], P('tm', 'head')
- ssd_out: bfloat16 [24576, 4096], P('tm', 'head')
Inputs may be any that keep to these rules, and one draw needn't show every extreme that they name: frame_ids is a permutation of the frames; the 12 slots of one tm index hold frames of 12 different time shards, time shard of a frame being frame // 12.
All inputs are finite; a program needn't handle non-finite values.
Results may differ from a plain program's by a relative error of at most 0.013.
Values may be sent and summed in bfloat16 or wider, within the bound.
No kernel may reach another device: no remote copies, remote signals or barrier semaphores. Data moves between devices by JAX's collectives and lax.ppermute only.
A program may use at most 128 MiB of HBM per device.

v0:
```python
import jax
import jax.numpy as jnp
from jax import lax
from jax.sharding import PartitionSpec as P

GRID = 16
POOL = 4
VHD = 72
HDIM = 64
STATE = 128
STRETCH = 256


highest = lax.Precision.HIGHEST


def carried_in(value, axis, combine, identity):
    count, position = (lax.axis_size(axis), lax.axis_index(axis))
    everything = jax.tree.map(
        lambda part, kind: lax.all_gather(part.astype(kind), axis),
        value,
        (jnp.bfloat16, jnp.bfloat16),
    )
    start = jax.tree.map(
        lambda part, zero: jnp.broadcast_to(jnp.asarray(zero, part.dtype), part.shape),
        value,
        identity,
    )

    def step(k, before):
        reached = k < position
        new = combine(
            before, jax.tree.map(lambda part, own: part[k].astype(own.dtype), everything, value)
        )
        return jax.tree.map(lambda a, b: jnp.where(reached, a, b), new, before)

    return lax.fori_loop(0, count, step, start)


def layer_norm(rows, gain):
    values = rows.astype(jnp.float32)
    centre = jnp.mean(values, axis=-1, keepdims=True)
    spread = jnp.mean(jnp.square(values - centre), axis=-1, keepdims=True)
    return ((values - centre) * lax.rsqrt(spread + 1e-06) * gain).astype(jnp.bfloat16)


def attend(full_patches, valid_count, ln_gain, w_qkv, w_out):
    frame_count, patch_count, full_width = full_patches.shape
    local_width = w_qkv.shape[2]
    local_heads = local_width // VHD
    normed = layer_norm(full_patches, ln_gain).reshape(frame_count * patch_count, full_width)
    triple = jnp.einsum("rc,mcd->mrd", normed, w_qkv, preferred_element_type=jnp.float32).astype(
        jnp.bfloat16
    )
    triple = triple.reshape(3, frame_count, patch_count, local_heads, VHD)
    scores = jnp.einsum(
        "fqhd,fkhd->fhqk", triple[0], triple[1], preferred_element_type=jnp.float32
    ) * VHD ** (-0.5)
    usable = jnp.arange(patch_count)[None, :] < valid_count[:, None]
    scores = jnp.where(usable[:, None, None, :], scores, -1e30)
    row_max = jnp.max(scores, axis=-1, keepdims=True)
    powered = jnp.exp(scores - row_max)
    weights_soft = (powered / jnp.sum(powered, axis=-1, keepdims=True)).astype(jnp.bfloat16)
    context = jnp.einsum(
        "fhqk,fkhd->fqhd", weights_soft, triple[2], preferred_element_type=jnp.float32
    ).astype(jnp.bfloat16)
    attended = jnp.dot(
        context.reshape(frame_count * patch_count, local_width),
        w_out,
        preferred_element_type=jnp.float32,
    )
    return jnp.mean(attended.reshape(frame_count, patch_count // POOL, POOL, full_width), axis=2)


def bucket_frames(owned, frame_ids, shards):
    frame_count = owned.shape[0]
    target = frame_ids // frame_count
    onehot = target[None, :] == jnp.arange(shards)[:, None]
    outgoing = jnp.einsum(
        "tf,fpc->tpc", onehot.astype(owned.dtype), owned, preferred_element_type=jnp.float32
    ).astype(owned.dtype)
    labels = jnp.sum(jnp.where(onehot, frame_ids[None, :] + 1, 0), axis=1)
    return (outgoing, labels)


def place_frames(incoming, arrived, frame_count):
    first_frame = lax.axis_index("tm") * frame_count
    local_frame = arrived - 1 - first_frame
    onehot = jnp.arange(frame_count)[:, None] == local_frame[None, :]
    placed = jnp.einsum(
        "ft,tpc->fpc", onehot.astype(incoming.dtype), incoming, preferred_element_type=jnp.float32
    ).astype(incoming.dtype)
    return placed.reshape(frame_count * incoming.shape[1], incoming.shape[2])


def project(stream_rows, norm_gain, w_x, w_b, w_c, w_dt, dt_bias, a_log):
    values = stream_rows.astype(jnp.float32)
    normed = (
        values * lax.rsqrt(jnp.mean(values * values, axis=-1, keepdims=True) + 1e-05) * norm_gain
    ).astype(jnp.bfloat16)
    inner_rows = jnp.dot(normed, w_x, preferred_element_type=jnp.float32).astype(jnp.bfloat16)
    write_keys = jnp.dot(normed, w_b, preferred_element_type=jnp.float32).astype(jnp.bfloat16)
    read_keys = jnp.dot(normed, w_c, preferred_element_type=jnp.float32).astype(jnp.bfloat16)
    step_size = jax.nn.softplus(jnp.dot(normed, w_dt, preferred_element_type=jnp.float32) + dt_bias)
    log_decay = -jnp.exp(a_log) * step_size
    return (inner_rows, write_keys, read_keys, step_size, log_decay)


def ssd_stretch(inner_rows, write_keys, read_keys, step_size, log_decay, d_skip, state):
    length = inner_rows.shape[0]
    head_count = step_size.shape[1]
    groups = write_keys.shape[1] // STATE
    per_group = head_count // groups
    cumul = jnp.cumsum(log_decay, axis=0)
    scaled = (
        inner_rows.astype(jnp.float32).reshape(length, head_count, HDIM) * step_size[:, :, None]
    )
    writers = write_keys.astype(jnp.float32).reshape(length, groups, STATE)
    readers = read_keys.astype(jnp.float32).reshape(length, groups, STATE)
    intersection = jnp.einsum("tgn,sgn->gts", readers, writers, precision=highest)
    causal = (jnp.arange(length)[:, None] >= jnp.arange(length)[None, :])[:, :, None]
    spans = cumul[:, None, :] - cumul[None, :, :]
    decays = jnp.where(causal, jnp.exp(jnp.where(causal, spans, 0.0)), 0.0)
    mixing = jnp.repeat(intersection, per_group, axis=0) * jnp.transpose(decays, (2, 0, 1))
    within = jnp.einsum("hts,shp->thp", mixing, scaled, precision=highest)
    carried = (
        jnp.einsum(
            "tgn,gkpn->tgkp",
            readers,
            state.reshape(groups, per_group, HDIM, STATE),
            precision=highest,
        ).reshape(length, head_count, HDIM)
        * jnp.exp(cumul)[:, :, None]
    )
    remaining = jnp.exp(cumul[-1][None, :] - cumul)
    fresh_state = jnp.einsum(
        "sgkp,sgn->gkpn",
        (scaled * remaining[:, :, None]).reshape(length, groups, per_group, HDIM),
        writers,
        precision=highest,
    ).reshape(head_count, HDIM, STATE)
    new_state = jnp.exp(cumul[-1])[:, None, None] * state + fresh_state
    outputs = (
        within
        + carried
        + d_skip[None, :, None] * inner_rows.astype(jnp.float32).reshape(length, head_count, HDIM)
    )
    return (outputs, new_state, cumul)


def group_norm(outputs, out_gain, groups):
    length = outputs.shape[0]
    grouped = outputs.reshape(length, groups, -1)
    normed = grouped * lax.rsqrt(jnp.mean(grouped * grouped, axis=-1, keepdims=True) + 1e-05)
    return (normed.reshape(length, -1) * out_gain).astype(jnp.bfloat16)


def combine_states(earlier, later):
    return (earlier[0] + later[0], jnp.exp(later[0])[:, None, None] * earlier[1] + later[1])


def on_device(
    patches,
    grid_rows,
    frame_ids,
    ln_gain,
    w_qkv,
    w_out,
    w_conn,
    norm_gain,
    w_x,
    w_b,
    w_c,
    w_dt,
    dt_bias,
    a_log,
    d_skip,
    out_gain,
):
    frame_count, patch_count, slice_width = patches.shape
    tokens_frame = patch_count // POOL
    shards = lax.axis_size("tm")
    full_patches = lax.all_gather(patches, "head", axis=2, tiled=True)
    full_width = full_patches.shape[2]
    valid_count = grid_rows * GRID
    attn_pooled = attend(full_patches, valid_count, ln_gain, w_qkv, w_out)
    kept_tokens = (jnp.arange(tokens_frame)[None, :] * POOL < valid_count[:, None])[:, :, None]
    summed_attn = lax.psum(attn_pooled, "head")
    pooled_patches = jnp.mean(
        full_patches.astype(jnp.float32).reshape(frame_count, tokens_frame, POOL, full_width),
        axis=2,
    )
    vision = jnp.where(kept_tokens, pooled_patches + summed_attn, 0.0).astype(jnp.bfloat16)
    projected = jnp.dot(
        vision.reshape(frame_count * tokens_frame, full_width),
        w_conn,
        preferred_element_type=jnp.float32,
    ).astype(jnp.bfloat16)
    outgoing, labels = bucket_frames(
        projected.reshape(frame_count, tokens_frame, w_conn.shape[1]), frame_ids, shards
    )
    incoming, arrived = (
        lax.all_to_all(outgoing, "tm", split_axis=0, concat_axis=0, tiled=True),
        lax.all_to_all(labels, "tm", split_axis=0, concat_axis=0, tiled=True),
    )
    stream_rows = place_frames(incoming, arrived, frame_count)
    wide = lax.all_gather(stream_rows, "head", axis=1, tiled=True)
    token_count = wide.shape[0]
    local_heads = w_dt.shape[1]
    groups = w_b.shape[1] // STATE
    per_group = local_heads // groups
    projected_rows = project(wide, norm_gain, w_x, w_b, w_c, w_dt, dt_bias, a_log)
    stretch_count = token_count // STRETCH
    sliced = tuple(
        (member.reshape(stretch_count, STRETCH, member.shape[1]) for member in projected_rows)
    )

    def stretch_step(state, pieces):
        outputs, new_state, cumul = ssd_stretch(
            pieces[0], pieces[1], pieces[2], pieces[3], pieces[4], d_skip, state
        )
        return (new_state, (outputs, cumul))

    zero_state = jnp.zeros((local_heads, HDIM, STATE), jnp.float32)
    device_state, (outputs, cumul) = lax.scan(stretch_step, zero_state, sliced)
    totals = cumul[:, -1, :]
    total_log = jnp.sum(totals, axis=0)
    identity = (jnp.zeros_like(total_log), jnp.zeros_like(device_state))
    incoming_state = carried_in((total_log, device_state), "tm", combine_states, identity)[1]
    offsets = jnp.cumsum(totals, axis=0) - totals
    from_start = (cumul + offsets[:, None, :]).reshape(token_count, local_heads)
    readers = projected_rows[2].astype(jnp.float32).reshape(token_count, groups, STATE)
    correction = (
        jnp.einsum(
            "tgn,gkpn->tgkp",
            readers,
            incoming_state.reshape(groups, per_group, HDIM, STATE),
            precision=highest,
        ).reshape(token_count, local_heads, HDIM)
        * jnp.exp(from_start)[:, :, None]
    )
    combined = outputs.reshape(token_count, local_heads, HDIM) + correction
    return (stream_rows, group_norm(combined, out_gain, groups))


def solution(mesh):
    in_specs = (
        P("tm", None, "head"),
        P("tm"),
        P("tm"),
        P(),
        P(None, None, "head"),
        P("head", None),
        P(None, "head"),
        P(),
        P(None, "head"),
        P(None, "head"),
        P(None, "head"),
        P(None, "head"),
        P("head"),
        P("head"),
        P("head"),
        P("head"),
    )
    out_specs = (P("tm", "head"), P("tm", "head"))
    return jax.shard_map(
        on_device, mesh=mesh, in_specs=in_specs, out_specs=out_specs, check_vma=False
    )
```

profile of v0, /device:TPU:32, one launch (start us, length us, event | category | flops | bytes accessed | tf_op | source)
XLA Modules:
  0.0 631.8 jit_solution(9153777899847162334)
XLA Ops:
  8.7 81.6 %all-gather.6.cloned.1.call-done = bf16[12,256,1152]{1,2,0:T(8,128)(2,1)} async-done(((bf16[12,256,144]{1,2,0:T(8,128)(2,1)}), bf16[12,256,1152]{1,2,0:T(8,128)(2,1)}) %all-gather.6.cloned.1.call-update) | async-done | bytes 7077904 | tf_op jit(solution)/shard_map/all_gather | solution.py:183
  90.3 10.3 %copy.77 = bf16[12,256,1152]{2,1,0:T(8,128)(2,1)} copy(bf16[12,256,1152]{1,2,0:T(8,128)(2,1)} %all-gather.6.cloned.1.call-done) | data formatting | bytes 14155776 | tf_op jit(solution)/shard_map/all_gather | solution.py:183
  100.7 4.2 convert_reduce_fusion
  110.2 3.6 fusion.80
  117.9 2.5 squeeze.31
  121.9 3.1 fusion.77
  127.0 3.5 copy.82
  130.5 2.6 dot_general.55
  133.1 3.8 convolution_reduce_fusion
  140.6 13.1 %all-to-all-start = ((s32[32,1,1]{2,1,0:T(1,128)}), s32[32,1,1]{2,1,0:T(1,128)S(1)}, u32[]{:S(2)}, u32[]{:S(2)}) async-start(s32[32,1,1]{2,1,0:T(1,128)} %copy.76), calls=%async_computation | async-start | bytes 32768 | tf_op jit(solution)/shard_map/all_to_all | solution.py:204
  153.8 13.9 %reshape.309 = f32[12,64,4,1152]{3,2,1,0:T(4,128)} reshape(bf16[12,256,1152]{2,1,0:T(8,128)(2,1)} %copy.77) | data formatting | bytes 21233664 | tf_op jit(solution)/shard_map/reshape | solution.py:190
  167.7 12.7 %reduce_sum.82 = f32[12,64,1152]{2,1,0:T(8,128)} reduce(f32[12,64,4,1152]{3,2,1,0:T(4,128)} %reshape.309, f32[]{:T(128)} %constant.94.clone.1), dimensions={2}, to_apply=%region_1.0 | reduce | flops 2654208 | bytes 17694724 | tf_op jit(solution)/shard_map/reduce_sum | solution.py:189
  180.4 54.9 %all-reduce.3.cloned.1.call-done = f32[12,64,1152]{2,1,0:T(8,128)} async-done(((f32[12,64,1152]{2,1,0:T(8,128)}), f32[12,64,1152]{2,1,0:T(8,128)}) %all-reduce.3.cloned.1.call-update) | async-done | bytes 3538960 | tf_op jit(solution)/shard_map/psum | solution.py:188
  235.3 3.5 select_convert_fusion
  240.8 2.5 copy.85
  243.4 13.3 %all-to-all-start.1 = ((bf16[32,64,512]{2,1,0:T(8,128)(2,1)}), bf16[32,64,512]{2,1,0:T(8,128)(2,1)S(1)}, u32[]{:S(2)}, u32[]{:S(2)}) async-start(bf16[32,64,512]{2,1,0:T(8,128)(2,1)} %copy.85), calls=%async_computation.1 | async-start | bytes 4194304 | tf_op jit(solution)/shard_map/all_to_all | solution.py:203
  257.4 52.7 %all-to-all-done.1 = bf16[32,64,512]{2,1,0:T(8,128)(2,1)S(1)} async-done(((bf16[32,64,512]{2,1,0:T(8,128)(2,1)}), bf16[32,64,512]{2,1,0:T(8,128)(2,1)S(1)}, u32[]{:S(2)}, u32[]{:S(2)}) %all-to-all-start.1) | async-done | bytes 2097184 | tf_op jit(solution)/shard_map/all_to_all | solution.py:203
  313.2 64.8 %all-gather.8.cloned.1.call-done = bf16[768,4096]{1,0:T(8,128)(2,1)} async-done(((bf16[768,512]{1,0:T(8,128)(2,1)}), bf16[768,4096]{1,0:T(8,128)(2,1)}) %all-gather.8.cloned.1.call-update) | async-done | bytes 6291472 | tf_op jit(solution)/shard_map/all_gather | solution.py:207
  378.0 4.2 fusion.38
  382.6 2.8 fusion.40
  385.4 6.6 %convolution_convert_fusion.1 = bf16[768,512]{1,0:T(8,128)(2,1)} fusion(bf16[768,4096]{1,0:T(8,128)(2,1)S(1)} %fusion.40, bf16[4096,512]{1,0:T(8,128)(2,1)} %param.28), kind=kOutput, calls=%fused_computation.84 | convolution fusion | flops 3221618688 | bytes 11272192 | tf_op jit(solution)/shard_map/dot_general | solution.py:101
  392.0 2.5 convolution_convert_fusion.4
  399.3 54.2 %while.29 = (s32[]{:T(128)}, f32[8,64,128]{2,1,0:T(8,128)S(1)}, f32[3,256,8,64]{1,0,3,2:T(4,128)S(1)}, f32[3,256,8]{1,2,0:T(8,128)}, f32[3,256,8]{1,2,0:T(8,128)...) while((s32[]{:T(128)}, f32[8,64,128]{2,1,0:T(8,128)S(1)}, ...), condition=%wide.region_12.13_spmd.clone, body=%wide.region_9.12_spmd.clone.sunk | while | flops 826087424 | bytes 8424928 | solution.py:225
  403.3 2.5 fusion.118
  407.7 7.5 %dynamic_update_slice.14 = f32[3,256,8,64]{1,0,3,2:T(4,128)S(1)} dynamic-update-slice(f32[3,256,8,64]{1,0,3,2:T(4,128)S(1)} %get-tuple-element.415, f32[1,256,8,64]{1,0,3,2:T(1,128)S(1)} %copy.125, s32[]{:T(128)} %get-tuple-element.413, s32[]{:T(128)} %constant.88.clone.1..sunk, s32[]{:T(128)} %constant.88.clone.1..sunk, s32[]{:T(128)} %constant.88.clone.1..sunk) | dynamic-update-slice | bytes 1048580 | tf_op jit(solution)/shard_map/while/body/jit(dynamic_update_index_in_dim)/dynamic_update_slice | solution.py:225
  421.3 2.5 fusion.118
  425.7 7.5 %dynamic_update_slice.14 = f32[3,256,8,64]{1,0,3,2:T(4,128)S(1)} dynamic-update-slice(f32[3,256,8,64]{1,0,3,2:T(4,128)S(1)} %get-tuple-element.415, f32[1,256,8,64]{1,0,3,2:T(1,128)S(1)} %copy.125, s32[]{:T(128)} %get-tuple-element.413, s32[]{:T(128)} %constant.88.clone.1..sunk, s32[]{:T(128)} %constant.88.clone.1..sunk, s32[]{:T(128)} %constant.88.clone.1..sunk) | dynamic-update-slice | bytes 1048580 | tf_op jit(solution)/shard_map/while/body/jit(dynamic_update_index_in_dim)/dynamic_update_slice | solution.py:225
  439.3 2.5 fusion.118
  443.6 7.5 %dynamic_update_slice.14 = f32[3,256,8,64]{1,0,3,2:T(4,128)S(1)} dynamic-update-slice(f32[3,256,8,64]{1,0,3,2:T(4,128)S(1)} %get-tuple-element.415, f32[1,256,8,64]{1,0,3,2:T(1,128)S(1)} %copy.125, s32[]{:T(128)} %get-tuple-element.413, s32[]{:T(128)} %constant.88.clone.1..sunk, s32[]{:T(128)} %constant.88.clone.1..sunk, s32[]{:T(128)} %constant.88.clone.1..sunk) | dynamic-update-slice | bytes 1048580 | tf_op jit(solution)/shard_map/while/body/jit(dynamic_update_index_in_dim)/dynamic_update_slice | solution.py:225
  458.5 121.4 %all-reduce = bf16[256]{0:T(256)(128)(2,1)S(1)} all-reduce(bf16[256]{0:T(256)(128)(2,1)S(1)} %dynamic-update-slice), channel_id=2, replica_groups=mesh['tm'=32,'head'=8] {'tm'}, use_global_device_ids=true, to_apply=%add | all-reduce | flops 256 | bytes 1024
  581.5 33.8 %while.30 = (s32[]{:T(128)}, f32[8,64,128]{2,1,0:T(8,128)S(1)}, s32[]{:T(128)}, bf16[32,8]{1,0:T(8,128)(2,1)S(1)}, bf16[32,8,64,128]{3,2,1,0:T(8,128)(2,1)}, /*index=5*/s32[]{:T(128)}, s32[]{:T(128)}) while((s32[]{:T(128)}, f32[8,64,128]{2,1,0:T(8,128)S(1)}, s32[]{:T(128)}, bf16[32,8]{1,0:T(8,128)(2,1)S(1)}, ...), condition=%wide.region_15.16_spmd.clone, body=%wide.region_14.15_spmd.clone.sunk | while | flops 327692 | bytes 655545 | solution.py:37
  618.9 3.1 multiply_reduce_fusion.1
  (221 shorter events, 98.0 us)
Async XLA Ops:
  7.2 231.7 %copy-start = (bf16[1152,512]{1,0:T(8,128)(2,1)S(1)}, bf16[1152,512]{1,0:T(8,128)(2,1)}, u32[]{:S(2)}) copy-start(bf16[1152,512]{1,0:T(8,128)(2,1)} %param.26) | copy-start | bytes 3538948
  7.2 83.1 %all-gather.6.cloned.1.call-start = ((), (), s32[]{:S(2)}) async-start(), calls=%async_computation.2 | async-start | bytes 7962624 | tf_op jit(solution)/shard_map/all_gather | solution.py:183
  7.9 227.4 %all-reduce.3.cloned.1.call-start = ((), (), s32[]{:S(2)}) async-start(), calls=%async_computation.3 | async-start | bytes 7077888 | tf_op jit(solution)/shard_map/psum | solution.py:188
  100.7 5.0 copy-start.2
  105.7 2.1 copy-start.10
  107.7 2.4 copy-start.15
  121.9 3.1 copy-start.5
  127.0 6.1 copy-start.16
  139.2 0.7 copy-start.17
  140.6 102.7 %all-to-all-start = ((s32[32,1,1]{2,1,0:T(1,128)}), s32[32,1,1]{2,1,0:T(1,128)S(1)}, u32[]{:S(2)}, u32[]{:S(2)}) async-start(s32[32,1,1]{2,1,0:T(1,128)} %copy.76), calls=%async_computation | async-start | bytes 32768 | tf_op jit(solution)/shard_map/all_to_all | solution.py:204
  243.4 66.7 %all-to-all-start.1 = ((bf16[32,64,512]{2,1,0:T(8,128)(2,1)}), bf16[32,64,512]{2,1,0:T(8,128)(2,1)S(1)}, u32[]{:S(2)}, u32[]{:S(2)}) async-start(bf16[32,64,512]{2,1,0:T(8,128)(2,1)} %copy.85), calls=%async_computation.1 | async-start | bytes 4194304 | tf_op jit(solution)/shard_map/all_to_all | solution.py:203
  256.7 56.5 %copy-start.18 = (f32[8]{0:T(128)S(1)}, f32[8]{0:T(128)}, u32[]{:S(2)}) copy-start(f32[8]{0:T(128)} %param.33) | copy-start | bytes 100
  256.7 121.3 %all-gather.8.cloned.1.call-start = ((), (), s32[]{:S(2)}) async-start(), calls=%async_computation.4 | async-start | bytes 7077888 | tf_op jit(solution)/shard_map/all_gather | solution.py:207
  312.9 69.4 %copy-start.8 = (f32[4096]{0:T(1024)S(1)}, f32[4096]{0:T(1024)}, u32[]{:S(2)}) copy-start(f32[4096]{0:T(1024)} %param.27) | copy-start | bytes 49156
  312.9 268.6 %all-gather.10.cloned.1.call-start = ((), (), s32[]{:S(2)}) async-start(), calls=%async_computation.5 | async-start | bytes 4325376 | tf_op jit(solution)/shard_map/all_gather | solution.py:20
  378.0 4.6 copy-start.3
  385.4 6.6 %copy-start.13 = (bf16[4096,128]{1,0:T(8,128)(2,1)S(1)}, bf16[4096,128]{1,0:T(8,128)(2,1)}, u32[]{:S(2)}) copy-start(bf16[4096,128]{1,0:T(8,128)(2,1)} %param.29) | copy-start | bytes 3145732
  392.0 2.5 copy-start.14
  394.5 2.5 copy-start.7
  394.5 2.5 copy-start.12
  396.9 2.4 copy-start.9
  399.3 54.9 %copy-start.19 = (u32[256]{0:T(256)S(1)}, u32[256]{0:T(256)}, u32[]{:S(2)}) copy-start(u32[256]{0:T(256)} %constant.109) | copy-start | bytes 3076
  453.5 128.0 %copy-start.4 = (f32[3,256,8,64]{1,0,3,2:T(4,128)}, f32[3,256,8,64]{1,0,3,2:T(4,128)S(1)}, u32[]{:S(2)}) copy-start(f32[3,256,8,64]{1,0,3,2:T(4,128)S(1)} %get-tuple-element.150) | copy-start | bytes 4718596
  457.3 124.2 %copy-start.6 = (f32[3,256,8]{1,2,0:T(8,128)}, f32[3,256,8]{1,2,0:T(8,128)S(1)}, u32[]{:S(2)}) copy-start(f32[3,256,8]{1,2,0:T(8,128)S(1)} %add_exponential_fusion) | copy-start | bytes 73732
  617.0 5.0 copy-start.11
  618.9 6.0 copy-start.1
Sparse Core Ops, SparseCore 0:
  9.8 80.4 all-gather.5
  139.3 95.8 all-reduce.2
  313.0 64.9 all-gather.7
  454.3 114.2 all-gather.9
where the time goes:
time: 644 us; the launch traced here: 632 us
  waiting for transfers between devices  255 us (40%)
  blocking collectives  121 us (19%)
  other arithmetic  84.9 us (13%)
  local copies, waits for them, and re-layouts  79.2 us (12%)
  matrix products  48.3 us (8%)
  starting transfers between devices  26.8 us (4%)
  between operations  15.2 us (2%)
    unnamed x1, blocking collectives  121 us
    all_gather x1, waiting for transfers between devices, on_device(): full_patches = lax.all_gather(patches, 'head', axis=2, tiled=True)  81.6 us
    all_gather x1, waiting for transfers between devices, on_device(): wide = lax.all_gather(stream_rows, 'head', axis=1, tiled=True)  64.8 us
    psum x1, waiting for transfers between devices, on_device(): summed_attn = lax.psum(attn_pooled, 'head')  54.9 us
    all_to_all x1, waiting for transfers between devices, on_device(): lax.all_to_all(outgoing, 'tm', split_axis=0, concat_axis=0, tiled=True)  52.7 us
    select_n x32, other arithmetic, step(): return jax.tree.map(lambda a, b: jnp.where(reached, a, b), new, before)  32.4 us
    dynamic_update_slice x6, local copies, waits for them, and re-layouts, on_device(): device_state, (outputs, cumul) = lax.scan(stretch_step, zero_state, sliced)  24.2 us
    reshape x1, local copies, waits for them, and re-layouts, on_device(): full_patches.astype(jnp.float32)  13.9 us
  transfers between devices with their start and end apart: 6, of which 4 were waited for; matrix products, arithmetic and copies ran while one was open for 7% of the time, Pallas kernels for 0%

commit v1 on v0

v1 whole, which is shorter than its diff:
```python
import functools
import jax
import jax.numpy as jnp
from jax import lax
from jax.experimental import pallas as pl
from jax.experimental.pallas import tpu as pltpu
from jax.sharding import Mesh, PartitionSpec as P

GRID = 16
POOL = 4
VHD = 72
HDIM = 64
STATE = 128
Q = 256
XW = 640

F32 = jnp.float32
BF16 = jnp.bfloat16
highest = lax.Precision.HIGHEST
VMEM_SPEC = pl.BlockSpec(memory_space=pltpu.VMEM)
SMEM_SPEC = pl.BlockSpec(memory_space=pltpu.SMEM)
ANY_SPEC = pl.BlockSpec(memory_space=pl.ANY)


def params(mib):
    return pltpu.CompilerParams(vmem_limit_bytes=mib * 2**20)


def dot(a, b, ca, cb, precision=None):
    return lax.dot_general(
        a, b, (((ca,), (cb,)), ((), ())), preferred_element_type=F32, precision=precision
    )


def ring_shift(value, axis, size, shift):
    return lax.ppermute(value, axis, [(i, (i + shift) % size) for i in range(size)])


def swap_core(value):
    return lax.ppermute(value, "c", [(0, 1), (1, 0)])


def gather_ring(block, axis):
    half = block.shape[0] // 2
    before = ring_shift(block, axis, 4, 1)
    after = ring_shift(block, axis, 4, -1)
    far_lo = ring_shift(before[:half], axis, 4, 1)
    far_hi = ring_shift(after[half:], axis, 4, -1)
    return (block, before, far_lo, far_hi, after)


def vision_kernel(place, rows, mine, other, gain, pool, *rest):
    weights = rest[:10]
    keep, give, wx, wy, qkv, ctx, sems = rest[10:]
    frame = pl.program_id(0)
    first = place[0] == 0

    def copies():
        made = []
        for member, (held, slot) in enumerate(((wx, 1), (wy, 2))):
            own, before, far_lo, far_hi, after = weights[5 * member : 5 * member + 5]
            for k, (source, lo, size) in enumerate(
                ((own, 0, 4), (before, 0, 4), (far_lo, 0, 2), (far_hi, 2, 2), (after, 0, 4))
            ):
                distance = (0, 1, 2, 2, 3)[k]
                index = lax.rem(place[slot] + 4 - distance, 4)
                made.append(
                    pltpu.make_async_copy(
                        source, held.at[index, pl.ds(lo, size)], sems.at[5 * member + k]
                    )
                )
        return made

    @pl.when(frame == 0)
    def _():
        for copy in copies():
            copy.start()

    parts = []
    for z in range(4):
        a, b = mine[z, 0].astype(F32), other[z, 0].astype(F32)
        parts.append(jnp.where(first, a, b))
        parts.append(jnp.where(first, b, a))
    x = jnp.concatenate(parts, axis=0)
    width = x.shape[0]
    centre = jnp.sum(x, axis=0, keepdims=True) * (1.0 / width)
    x = x - centre
    spread = jnp.sum(x * x, axis=0, keepdims=True) * (1.0 / width)
    normed = (x * lax.rsqrt(spread + 1e-06) * gain[...]).astype(BF16)

    @pl.when(frame == 0)
    def _():
        for copy in copies():
            copy.wait()

    for m in range(3):
        left = wx[m].reshape(576, XW)
        right = wy[m].reshape(576, width - XW)
        qkv[m] = dot(left, normed[:XW], 1, 0) + dot(right, normed[XW:], 1, 0)
    valid = rows[frame] * GRID
    usable = lax.broadcasted_iota(jnp.int32, (256, 256), 0) < valid
    for h in range(8):
        span = pl.ds(h * VHD, VHD)
        q, k, v = (qkv[m, span, :].astype(BF16) for m in range(3))
        scores = dot(k, q, 0, 0) * VHD ** (-0.5)
        scores = jnp.where(usable, scores, -1e30)
        top = jnp.max(scores, axis=0, keepdims=True)
        powered = jnp.exp(scores - top)
        total = jnp.sum(powered, axis=0, keepdims=True)
        ctx[span, :] = dot(v, powered.astype(BF16), 1, 0) * (1.0 / total)
    pooled = dot(ctx[...].astype(BF16), pool[...], 1, 0)
    high = pooled.astype(BF16)
    low = (pooled - high.astype(F32)).astype(BF16)
    both = jnp.concatenate([high, low], axis=1)
    out_x = dot(both, wx[3].reshape(576, XW), 0, 0)
    out_y = dot(both, wy[3].reshape(576, width - XW), 0, 0)
    attended = jnp.concatenate([out_x, out_y], axis=1)
    attended = (attended[:64] + attended[64:]).T
    for z in range(4):
        a = attended[(2 * z) * 144 : (2 * z + 1) * 144]
        b = attended[(2 * z + 1) * 144 : (2 * z + 2) * 144]
        own = jnp.where(first, a, b) + dot(mine[z, 0], pool[...], 1, 0)
        far = jnp.where(first, b, a)
        keep[z, 0] = jnp.concatenate([own[:72], own[72:]], axis=1)
        give[z, 0] = jnp.concatenate([far[:72], far[72:]], axis=1)


def vision(place, rows, mine, other, ln_gain, pool, wx, wy):
    part = pl.BlockSpec((4, 1, 144, 256), lambda f: (0, f, 0, 0))
    out = pl.BlockSpec((4, 1, 72, 128), lambda f: (0, f, 0, 0))
    shape = jax.ShapeDtypeStruct((4, 3, 72, 128), F32)
    return pl.pallas_call(
        vision_kernel,
        grid=(3,),
        in_specs=[SMEM_SPEC, SMEM_SPEC, part, part, VMEM_SPEC, VMEM_SPEC] + [ANY_SPEC] * 10,
        out_specs=(out, out),
        out_shape=(shape, shape),
        scratch_shapes=[
            pltpu.VMEM((4, 4, 144, XW), BF16),
            pltpu.VMEM((4, 4, 144, 1152 - XW), BF16),
            pltpu.VMEM((3, 576, 256), F32),
            pltpu.VMEM((576, 256), F32),
            pltpu.SemaphoreType.DMA((10,)),
        ],
        compiler_params=params(48),
        name="vision",
    )(place, rows, mine, other, ln_gain, pool, *wx, *wy)


def bucket_kernel(target, seen, out):
    out[...] = jnp.zeros_like(out)
    for f in range(12):
        out[target[f]] = seen[f]


def bucket(target, seen):
    return pl.pallas_call(
        bucket_kernel,
        in_specs=[SMEM_SPEC, VMEM_SPEC],
        out_specs=VMEM_SPEC,
        out_shape=jax.ShapeDtypeStruct((32, 72, 128), BF16),
        compiler_params=params(16),
        name="bucket",
    )(target, seen)


def place_kernel(source, incoming, out):
    left = lax.broadcasted_iota(jnp.int32, (72, 128), 1) < 64
    for pair in range(6):
        a = incoming[source[2 * pair]].astype(F32)
        b = incoming[source[2 * pair + 1]].astype(F32)
        lanes = pl.ds(128 * pair, 128)
        top = jnp.where(left, a, pltpu.roll(b, 64, 1))
        bottom = jnp.where(left, pltpu.roll(a, 64, 1), b)
        out[:, lanes] = jnp.concatenate([top, bottom], axis=0).astype(BF16)


def place_frames(source, incoming):
    return pl.pallas_call(
        place_kernel,
        in_specs=[SMEM_SPEC, VMEM_SPEC],
        out_specs=VMEM_SPEC,
        out_shape=jax.ShapeDtypeStruct((144, 768), BF16),
        compiler_params=params(16),
        name="place",
    )(source, incoming)


def stream_kernel(place, mine, other, w_conn, stream, seen, squares):
    first = place[0] == 0
    for z in range(4):
        a, b = mine[z], other[z]
        seen[pl.ds(288 * z, 144), :] = jnp.where(first, a, b)
        seen[pl.ds(288 * z + 144, 144), :] = jnp.where(first, b, a)
    made = dot(w_conn[...], seen[...], 0, 0).astype(BF16)
    wide = made.astype(F32)
    squares[...] = jnp.broadcast_to(
        jnp.sum(wide * wide, axis=0, keepdims=True), squares.shape
    )
    stream[...] = wide.T.astype(BF16)


def stream_rows(place, mine, other, w_conn):
    tokens, width = mine.shape[2], w_conn.shape[1]
    return pl.pallas_call(
        stream_kernel,
        in_specs=[SMEM_SPEC, VMEM_SPEC, VMEM_SPEC, VMEM_SPEC],
        out_specs=(VMEM_SPEC, VMEM_SPEC, VMEM_SPEC),
        out_shape=(
            jax.ShapeDtypeStruct((tokens, width), BF16),
            jax.ShapeDtypeStruct((1152, tokens), BF16),
            jax.ShapeDtypeStruct((8, tokens), F32),
        ),
        compiler_params=params(40),
        name="stream",
    )(place, mine, other, w_conn)


def over_heads(rows, length):
    return jnp.concatenate(
        [jnp.broadcast_to(rows[h : h + 1], (HDIM, length)) for h in range(8)], axis=0
    )


def triangle(transposed):
    a = lax.broadcasted_iota(jnp.int32, (Q, Q), 0)
    b = lax.broadcasted_iota(jnp.int32, (Q, Q), 1)
    return jnp.where(a >= b if transposed else a <= b, 1.0, 0.0).astype(F32)


def state_kernel(
    seen, wide, squares, bias, a_log, inner, writers, readers, steps, logs, enter, payload
):
    raw = dot(wide[...], seen[...], 1, 0)
    scale = lax.rsqrt(jnp.sum(squares[...], axis=0) * (1.0 / 4096) + 1e-05)
    scale = scale[0:1]
    inner[...] = (raw[:512] * scale).astype(BF16)
    writers[...] = (raw[512:640] * scale).astype(BF16)
    readers[...] = (raw[640:768] * scale).astype(BF16)
    before = raw[768:776] * scale + bias[:, :1]
    step = jnp.maximum(before, 0.0) + jnp.log1p(jnp.exp(-jnp.abs(before)))
    log = -jnp.exp(a_log[:, :1]) * step
    steps[...] = step
    logs[...] = log
    upper = triangle(False)
    count = seen.shape[1] // Q
    state = jnp.zeros((512, STATE), F32)
    whole = jnp.zeros((8, 1), F32)
    for n in range(count):
        lanes = slice(n * Q, (n + 1) * Q)
        cumul = dot(log[:, lanes], upper, 1, 0, highest)
        total = cumul[:, Q - 1 : Q]
        enter[n] = state.astype(BF16)
        left = over_heads(step[:, lanes] * jnp.exp(total - cumul), Q)
        scaled = (inner[:, lanes].astype(F32) * left).astype(BF16)
        fresh = dot(scaled, writers[:, lanes], 1, 1)
        state = state * over_heads(jnp.broadcast_to(jnp.exp(total), (8, STATE)), STATE) + fresh
        whole = whole + total
    payload[pl.ds(0, 512), :] = state
    payload[pl.ds(512, 8), :] = jnp.broadcast_to(jnp.exp(whole), (8, STATE))


def local_states(seen, wide, squares, bias, a_log):
    tokens = seen.shape[1]
    return pl.pallas_call(
        state_kernel,
        in_specs=[VMEM_SPEC] * 5,
        out_specs=(VMEM_SPEC,) * 7,
        out_shape=(
            jax.ShapeDtypeStruct((512, tokens), BF16),
            jax.ShapeDtypeStruct((STATE, tokens), BF16),
            jax.ShapeDtypeStruct((STATE, tokens), BF16),
            jax.ShapeDtypeStruct((8, tokens), F32),
            jax.ShapeDtypeStruct((8, tokens), F32),
            jax.ShapeDtypeStruct((tokens // Q, 512, STATE), BF16),
            jax.ShapeDtypeStruct((520, STATE), F32),
        ),
        compiler_params=params(40),
        name="states",
    )(seen, wide, squares, bias, a_log)


def within_kernel(inner, writers, readers, steps, logs, enter, d_skip, out, begun):
    upper, lower = triangle(False), triangle(True)
    causal = upper > 0.0
    whole = jnp.zeros((8, 1), F32)
    for n in range(inner.shape[1] // Q):
        lanes = slice(n * Q, (n + 1) * Q)
        log = logs[:, lanes]
        cumul = dot(log, upper, 1, 0, highest)
        column = dot(lower, log, 1, 1, highest)
        begun[:, lanes] = cumul + whole
        whole = whole + cumul[:, Q - 1 : Q]
        meets = dot(writers[:, lanes], readers[:, lanes], 0, 0)
        carried = dot(enter[n], readers[:, lanes], 1, 0)
        grown = jnp.exp(cumul)
        step = steps[:, lanes]
        for h in range(8):
            span = slice(h * HDIM, (h + 1) * HDIM)
            apart = jnp.minimum(cumul[h : h + 1] - column[:, h : h + 1], 0.0)
            mixing = jnp.where(causal, meets * jnp.exp(apart), 0.0).astype(BF16)
            own = inner[span, lanes].astype(F32)
            scaled = (own * step[h : h + 1]).astype(BF16)
            out[span, lanes] = (
                dot(scaled, mixing, 1, 0)
                + carried[span] * grown[h : h + 1]
                + d_skip[span] * own
            )


def within(inner, writers, readers, steps, logs, enter, d_skip):
    tokens = inner.shape[1]
    return pl.pallas_call(
        within_kernel,
        in_specs=[VMEM_SPEC] * 7,
        out_specs=(VMEM_SPEC,) * 2,
        out_shape=(
            jax.ShapeDtypeStruct((512, tokens), F32),
            jax.ShapeDtypeStruct((8, tokens), F32),
        ),
        compiler_params=params(40),
        cost_estimate=pl.CostEstimate(
            flops=2_000_000_000, bytes_accessed=6_000_000, transcendentals=2_000_000
        ),
        name="within",
    )(inner, writers, readers, steps, logs, enter, d_skip)


def finish_kernel(local, begun, readers, state, gain, out):
    for n in range(local.shape[1] // Q):
        lanes = slice(n * Q, (n + 1) * Q)
        carried = dot(state[...], readers[:, lanes], 1, 0)
        y = local[:, lanes] + carried * over_heads(jnp.exp(begun[:, lanes]), Q)
        mean = jnp.sum(y * y, axis=0, keepdims=True) * (1.0 / 512)
        y = y * lax.rsqrt(mean + 1e-05) * gain[...]
        out[lanes, :] = y.T.astype(BF16)


def finish(local, begun, readers, state, gain):
    return pl.pallas_call(
        finish_kernel,
        in_specs=[VMEM_SPEC] * 5,
        out_specs=VMEM_SPEC,
        out_shape=jax.ShapeDtypeStruct((local.shape[1], 512), BF16),
        compiler_params=params(40),
        name="finish",
    )(local, begun, readers, state, gain)


def split_payload(payload):
    payload = payload.astype(F32)
    return payload[:512].reshape(8, HDIM, STATE), payload[512:].reshape(8, 1, STATE)


def pass_along(payload, axis, size):
    position = lax.axis_index(axis)
    sent = payload.astype(BF16)
    got = [split_payload(ring_shift(sent, axis, size, k)) for k in range(1, size)]
    own = split_payload(payload)
    ahead, shrink = jnp.zeros_like(own[0]), jnp.ones_like(own[1])
    for k in range(1, size):
        state, decay = got[k - 1]
        here = position >= k
        ahead = jnp.where(here, ahead + shrink * state, ahead)
        shrink = jnp.where(here, shrink * decay, shrink)
    total, left = ahead * own[1] + own[0], shrink * own[1]
    for k in range(size - 1, 0, -1):
        state, decay = got[k - 1]
        here = position < k
        total = jnp.where(here, total * decay + state, total)
        left = jnp.where(here, left * decay, left)
    joined = jnp.concatenate([total.reshape(512, STATE), left.reshape(8, STATE)], axis=0)
    return ahead, shrink, joined


def on_device(
    patches, grid_rows, frame_ids, ln_gain, w_qkv, w_out, w_conn, norm_gain,
    w_x, w_b, w_c, w_dt, dt_bias, a_log, d_skip, out_gain,
):
    core, x, y, zl, zh = (lax.axis_index(a) for a in ("c", "x", "y", "zl", "zh"))
    shard = zh * 16 + y * 4 + x
    place = jnp.stack([core, x, y]).astype(jnp.int32)

    block = jnp.concatenate([jnp.transpose(w_qkv, (0, 2, 1)), w_out[None]], axis=0)
    piece_x = lax.dynamic_slice(block, (x, 0, 0), (1, 144, 1152))[:, :, :XW]
    piece_y = lax.dynamic_slice(block, (y, 0, 0), (1, 144, 1152))[:, :, XW:]
    gathered = []
    for piece, axis in ((piece_x, "x"), (piece_y, "y")):
        stacked = jnp.concatenate(
            [piece] + [ring_shift(piece, "zl", 4, k) for k in (1, 2, 3)], axis=0
        )
        gathered.append(gather_ring(stacked, axis))

    turned = jnp.transpose(patches, (0, 2, 1))
    mine = lax.all_to_all(turned, "zl", split_axis=0, concat_axis=0, tiled=True)
    other = swap_core(mine)
    mine, other = mine.reshape(4, 3, 144, 256), other.reshape(4, 3, 144, 256)

    all_ids = lax.all_gather(frame_ids, ("zh", "y", "x"), axis=0, tiled=True)
    wanted = shard * 12 + jnp.arange(12)
    source = jnp.sum(
        jnp.where(all_ids[None, :] == wanted[:, None], jnp.arange(384)[None, :] // 12, 0), axis=1
    ).astype(jnp.int32)

    own_rows = lax.dynamic_slice(w_conn, ((y * 4 + x) * 72, 0), (72, 512))
    full_rows = lax.all_gather(own_rows, ("zl", "c"), axis=1, tiled=True).astype(F32) * norm_gain
    high = full_rows.astype(BF16)
    low = (full_rows - high.astype(F32)).astype(BF16)
    both = jnp.concatenate([high, low], axis=0)
    products = [dot(both, w, 1, 0) for w in (w_x, w_b, w_c, w_dt)]
    product = jnp.concatenate([p[:72] + p[72:] for p in products], axis=1)
    product = jnp.pad(product, ((0, 0), (0, 120))).astype(BF16)
    wide = lax.all_gather(product, ("y", "x"), axis=0, tiled=True).T

    pool = (
        jnp.where(jnp.arange(256)[:, None] // POOL == jnp.arange(64)[None, :], 1.0 / POOL, 0.0)
    ).astype(BF16)
    own_frames = lax.dynamic_slice(grid_rows, (zl * 3,), (3,))
    keep, give = vision(
        place, own_frames, mine, other, ln_gain[:, None], pool, gathered[0], gathered[1]
    )
    summed = keep + swap_core(give)
    token = jnp.arange(128) % 64
    kept = token[None, :] * POOL < (own_frames * GRID)[:, None]
    seen = jnp.where(kept[None, :, None, :], summed, 0.0).astype(BF16)
    seen = lax.all_to_all(seen.reshape(12, 72, 128), "zl", split_axis=0, concat_axis=0, tiled=True)

    outgoing = bucket(frame_ids // 12, seen)
    incoming = lax.all_to_all(
        outgoing, ("zh", "y", "x"), split_axis=0, concat_axis=0, tiled=True
    )
    own_features = place_frames(source, incoming)
    line = lax.all_gather(own_features, "zl", axis=0)
    stream, features, squares = stream_rows(place, line, swap_core(line), w_conn)
    squares = lax.all_gather(squares, ("zl", "c"), axis=0)

    def column(values, repeat):
        return jnp.broadcast_to(values[:, None], (values.shape[0], repeat))

    inner, writers, readers, steps, logs, enter, payload = local_states(
        features, wide, squares, column(dt_bias, 128), column(a_log, 128)
    )
    local, begun = within(
        inner, writers, readers, steps, logs, enter, jnp.repeat(d_skip, HDIM)[:, None]
    )
    ahead_x, shrink_x, row = pass_along(payload, "x", 4)
    ahead_y, shrink_y, plane = pass_along(row, "y", 4)
    ahead_z = pass_along(plane, "zh", 2)[0]
    state = ahead_x + shrink_x * (ahead_y + shrink_y * ahead_z)
    mixed = finish(
        local, begun, readers, state.reshape(512, STATE).astype(BF16), out_gain[:, None]
    )
    return stream, mixed


def solution(mesh):
    fine = Mesh(mesh.devices.reshape(2, 4, 4, 4, 2), ("zh", "y", "x", "zl", "c"))
    tm, head = ("zh", "y", "x"), ("zl", "c")
    in_specs = (
        P(tm, None, head),
        P(tm),
        P(tm),
        P(),
        P(None, None, head),
        P(head, None),
        P(None, head),
        P(),
        P(None, head),
        P(None, head),
        P(None, head),
        P(None, head),
        P(head),
        P(head),
        P(head),
        P(head),
    )
    out_specs = (P(tm, head), P(tm, head))
    return jax.shard_map(
        on_device, mesh=fine, in_specs=in_specs, out_specs=out_specs, check_vma=False
    )
```

time: 644 us -> 276 us (0.43); the launches traced: 632 us -> 275 us
  waiting for transfers between devices: 255 us -> 47.6 us
  other arithmetic: 84.9 us -> 11.5 us
  local copies, waits for them, and re-layouts: 79.2 us -> 16.3 us
  matrix products: 48.3 us -> 2.79 us
  Pallas kernels: 0 us -> 32.2 us
  starting transfers between devices: 26.8 us -> 52.1 us
  blocking collectives: 121 us -> 97.3 us
    all_gather x3 -> x1, waiting for transfers between devices: 146 us -> 0.01 us  [on_device(): wide = lax.all_gather(product, ('y', 'x'), axis=0, tiled=True).T]
    unnamed x1, blocking collectives: 121 us -> 23.8 us
    all_gather x0 -> x3, blocking collectives: none -> 73.4 us  [the longest x1 41.7 us: on_device(): lax.all_gather(own_rows, ('zl', 'c'), axis=1, tiled=True).astype(F32)]
    psum x1 -> x0, waiting for transfers between devices: 54.9 us -> none  [on_device(): summed_attn = lax.psum(attn_pooled, 'head')]
    all_to_all x2 -> x3, waiting for transfers between devices: 52.7 us -> 6.64 us  [the longest x1 6.63 us: on_device(): lax.all_to_all(seen.reshape(12, 72, 128), 'zl', split_axis=0, concat_axis...]
    dot_general x23 -> x4, matrix products: 44.7 us -> 2.79 us  [dot(): lax.dot_general(a, b, (((ca,), (cb,)), ((), ())), preferred_element_type=...]
    ppermute x0 -> x24, waiting for transfers between devices: none -> 41 us  [the longest x21 39.3 us: ring_shift(): lax.ppermute(value, axis, [(i, (i + shift) % size) for i in range(size)])]
    select_n x32 -> x4, other arithmetic: 32.4 us -> 0.04 us  [the longest x1 0.02 us: pass_along(): shrink = jnp.where(here, shrink * decay, shrink)]
  transfers between devices with their start and end apart: 6 -> 28, of which waited for: 4 -> 13; matrix products, arithmetic and copies ran while one was open for 7% -> 6% of each run, Pallas kernels for 0% -> 9%
where the time goes in v1:
time: 276 us; the launch traced here: 275 us
  blocking collectives  97.3 us (35%)
  starting transfers between devices  52.1 us (19%)
  waiting for transfers between devices  47.6 us (17%)
  Pallas kernels  32.2 us (12%)
  local copies, waits for them, and re-layouts  16.3 us (6%)
  between operations  15.2 us (6%)
  other arithmetic  11.5 us (4%)
  matrix products  2.79 us (1%)
    all_gather x1, blocking collectives, on_device(): lax.all_gather(own_rows, ('zl', 'c'), axis=1, tiled=True).astype(F32)  41.7 us
    ppermute x21, waiting for transfers between devices, ring_shift(): lax.ppermute(value, axis, [(i, (i + shift) % size) for i in range(size)])  39.3 us
    ppermute x21, starting transfers between devices, ring_shift(): lax.ppermute(value, axis, [(i, (i + shift) % size) for i in range(size)])  30.3 us
    unnamed x1, blocking collectives  23.8 us
    pallas_call x1, Pallas kernels, vision(): pl.pallas_call(vision_kernel, grid=(3,), in_specs=[SMEM_SPEC, SMEM_SPEC,...  18.6 us
    all_gather x1, blocking collectives, on_device(): line = lax.all_gather(own_features, 'zl', axis=0)  17.1 us
    all_gather x1, blocking collectives, on_device(): squares = lax.all_gather(squares, ('zl', 'c'), axis=0)  14.6 us
    all_to_all x1, starting transfers between devices, on_device(): lax.all_to_all(outgoing, ('zh', 'y', 'x'), split_axis=0, concat_axis=0, t...  9.17 us
  transfers between devices with their start and end apart: 28, of which 13 were waited for; matrix products, arithmetic and copies ran while one was open for 6% of the time, Pallas kernels for 9%

profile of v1, /device:TPU:32, one launch (start us, length us, event | category | flops | bytes accessed | tf_op | source)
XLA Modules:
  0.0 274.9 jit_solution(9533188840480653762)
XLA Ops:
  8.4 1.9 collective-permute-start.3
  11.8 2.8 %collective-permute-start.1 = (bf16[1,144,640]{2,1,0:T(8,128)(2,1)S(1)}, bf16[1,144,640]{2,1,0:T(8,128)(2,1)}, u32[]{:S(2)}, u32[]{:S(2)}) collective-permute-start(bf16[1,144,640]{2,1,0:T(8,128)(2,1)S(1)} %fusion.24), channel_id=1, source_target_pairs={{0,2},{2,4},{4,6},{6,0},{1,3},{3,5},{5,7},{7,1},{8,10},{10,12},{12... | collective-permute-start | bytes 552968 | tf_op jit(solution)/shard_map/ppermute | solution.py:36
  16.3 6.2 %all-to-all-start = ((bf16[12,144,256]{2,1,0:T(8,128)(2,1)}), bf16[12,144,256]{2,1,0:T(8,128)(2,1)}, u32[]{:S(2)}, u32[]{:S(2)}) async-start(bf16[12,144,256]{2,1,0:T(8,128)(2,1)} %bitcast.4), calls=%async_computation | async-start | bytes 1769472 | tf_op jit(solution)/shard_map/all_to_all | solution.py:395
  23.4 41.7 %all_gather.24 = bf16[72,4096]{1,0:T(8,128)(2,1)S(1)} all-gather(bf16[72,512]{1,0:T(8,128)(2,1)S(1)} %constant_dynamic-slice_fusion), channel_id=1, replica_groups=mesh['zh'=2,'y'=4,'x'=4,'zl'=4,'c'=2] {'zl','c'}, dimensions={1}, use_global_device_ids=true | all-gather | bytes 663552 | tf_op jit(solution)/shard_map/all_gather | solution.py:406
  69.6 2.8 %collective-permute-start.8 = (bf16[1,144,512]{2,1,0:T(8,128)(2,1)S(1)}, bf16[1,144,512]{2,1,0:T(8,128)(2,1)S(1)}, u32[]{:S(2)}, u32[]{:S(2)}) collective-permute-start(bf16[1,144,512]{2,1,0:T(8,128)(2,1)S(1)} %fusion.25), channel_id=1, source_target_pairs={{0,2},{2,4},{4,6},{6,0},{1,3},{3,5},{5,7},{7,1},{8,10},{10,12},{12... | collective-permute-start | bytes 442376 | tf_op jit(solution)/shard_map/ppermute | solution.py:36
  75.0 1.7 collective-permute-start.6
  78.6 1.7 collective-permute-start.11
  80.3 1.7 collective-permute-start.13
  84.2 9.0 %collective-permute-done.4.rest_1_ = bf16[4,144,640]{2,1,0:T(8,128)(2,1)S(1)} collective-permute-done((bf16[4,144,640]{2,1,0:T(8,128)(2,1)S(1)}, bf16[4,144,640]{2,1,0:T(8,128)(2,1)S(1)}, u32[]{:S(2)}, u32[]{:S(2)}) %collective-permute-start.4) | collective-permute-done | bytes 737312 | tf_op jit(solution)/shard_map/ppermute | solution.py:36
  94.6 3.2 %collective-permute-start.7 = (bf16[2,144,640]{2,1,0:T(8,128)(2,1)S(1)}, bf16[2,144,640]{2,1,0:T(8,128)(2,1)S(1)}, u32[]{:S(2)}, u32[]{:S(2)}) collective-permute-start(bf16[2,144,640]{2,1,0:T(8,128)(2,1)S(1)} %slice.121), channel_id=1, source_target_pairs={{0,24},{8,0},{16,8},{24,16},{1,25},{9,1},{17,9},{25,17},{2,26},{10... | collective-permute-start | bytes 1105928 | tf_op jit(solution)/shard_map/ppermute | solution.py:36
  99.1 1.7 collective-permute-start.12
  101.7 1.8 collective-permute-start.14
  103.6 5.9 %collective-permute-done.12.rest_7_ = bf16[2,144,512]{2,1,0:T(8,128)(2,1)S(1)} collective-permute-done((bf16[2,144,512]{2,1,0:T(8,128)(2,1)S(1)}, bf16[2,144,512]{2,1,0:T(8,128)(2,1)S(1)}, u32[]{:S(2)}, u32[]{:S(2)}) %collective-permute-start.12) | collective-permute-done | bytes 294944 | tf_op jit(solution)/shard_map/ppermute | solution.py:36
  110.0 18.6 %vision.1 = (f32[4,3,72,128]{3,2,1,0:T(8,128)S(1)}, f32[4,3,72,128]{3,2,1,0:T(8,128)S(1)}) custom-call(s32[3]{0:T(128)S(1)} %get-tuple-element.46.place, s32[3]{0:T(128)S(1)} %get-tuple-element.35.rows, bf16[4,3,144,256]{3,2,1,0:T(8,128)(2,1)} %bitcast.5.mine, bf16[4,3,144,256]{3,2,1,0:T(8,128)(2,1)} %bitcast.6.other, f32[1152,1]{1,0:T(8,128)S(1)} %broadcast_in_dim.77.gain, ...), custom_call_target="tpu_custom_call" | custom-call | tf_op jit(solution)/shard_map/vision/pallas_call | solution.py:132
  128.8 1.7 collective-permute-done.15
  131.3 6.3 %all-to-all-start.1 = ((bf16[12,72,128]{2,1,0:T(8,128)(2,1)}), bf16[12,72,128]{2,1,0:T(8,128)(2,1)S(1)}, u32[]{:S(2)}, u32[]{:S(2)}) async-start(bf16[12,72,128]{2,1,0:T(8,128)(2,1)} %bitcast.9), calls=%async_computation.1 | async-start | bytes 442368 | tf_op jit(solution)/shard_map/all_to_all | solution.py:426
  137.6 6.6 %all-to-all-done.1.seen = bf16[12,72,128]{2,1,0:T(8,128)(2,1)S(1)} async-done(((bf16[12,72,128]{2,1,0:T(8,128)(2,1)}), bf16[12,72,128]{2,1,0:T(8,128)(2,1)S(1)}, u32[]{:S(2)}, u32[]{:S(2)}) %all-to-all-start.1) | async-done | bytes 221216 | tf_op jit(solution)/shard_map/all_to_all | solution.py:426
  145.7 9.2 %all-to-all-start.2 = ((bf16[32,72,128]{2,1,0:T(8,128)(2,1)}), bf16[32,72,128]{2,1,0:T(8,128)(2,1)S(1)}, u32[]{:S(2)}, u32[]{:S(2)}) async-start(bf16[32,72,128]{2,1,0:T(8,128)(2,1)} %bucket.1), calls=%async_computation.2 | async-start | bytes 1179648 | tf_op jit(solution)/shard_map/all_to_all | solution.py:429
  156.5 23.8 %all-reduce.1 = s32[384]{0:T(512)S(1)} all-reduce(s32[384]{0:T(512)S(1)} %dynamic-update-slice), channel_id=1, replica_groups=mesh['zh'=2,'y'=4,'x'=4,'zl'=4,'c'=2] {'zh','y','x'}, use_global_device_ids=true, to_apply=%add.1 | all-reduce | flops 384 | bytes 3072
  181.2 17.1 %all-gather = bf16[576,768]{1,0:T(8,128)(2,1)} all-gather(bf16[144,768]{1,0:T(8,128)(2,1)S(1)} %place.1), channel_id=2, replica_groups=mesh['zh'=2,'y'=4,'x'=4,'zl'=4,'c'=2] {'zl'}, dimensions={0}, use_global_device_ids=true | all-gather | bytes 1105920 | tf_op jit(solution)/shard_map/all_gather | solution.py:433
  198.3 2.9 %copy.42 = bf16[1152,896]{0,1:T(8,128)(2,1)S(1)} copy(bf16[1152,896]{1,0:T(8,128)(2,1)} %all-gather.4.cloned.1.call-done) | data formatting | bytes 4128768 | tf_op jit(solution)/shard_map/all_gather | solution.py:413
  202.5 3.7 %stream.1 = (bf16[768,512]{1,0:T(8,128)(2,1)}, bf16[1152,768]{1,0:T(8,128)(2,1)S(1)}, f32[8,768]{1,0:T(8,128)S(1)}) custom-call(s32[3]{0:T(128)S(1)} %get-tuple-element.46.place, bf16[4,144,768]{2,1,0:T(8,128)(2,1)} %bitcast.10.mine, bf16[4,144,768]{2,1,0:T(8,128)(2,1)} %collective-permute-done.16.other, bf16[1152,512]{1,0:T(8,128)(2,1)S(1)} %copy-done.1), custom_call_target="tpu_custom_call" | custom-call | tf_op jit(solution)/shard_map/stream/pallas_call | solution.py:205
  206.3 14.6 %all-gather.1 = f32[64,768]{1,0:T(8,128)S(1)} all-gather(f32[8,768]{1,0:T(8,128)S(1)} %get-tuple-element.20), channel_id=3, replica_groups=mesh['zh'=2,'y'=4,'x'=4,'zl'=4,'c'=2] {'zl','c'}, dimensions={0}, use_global_device_ids=true | all-gather | bytes 221184 | tf_op jit(solution)/shard_map/all_gather | solution.py:435
  221.0 3.1 %states.1 = (bf16[512,768]{1,0:T(8,128)(2,1)S(1)}, bf16[128,768]{1,0:T(8,128)(2,1)S(1)}, bf16[128,768]{1,0:T(8,128)(2,1)S(1)}, f32[8,768]{1,0:T(8,128)S(1)}, f32...) custom-call(bf16[1152,768]{1,0:T(8,128)(2,1)S(1)} %get-tuple-element.19.seen, ...), custom_call_target="tpu_custom_call" | custom-call | tf_op jit(solution)/shard_map/states/pallas_call | solution.py:265
  229.6 3.9 %collective-permute-done.19 = bf16[520,128]{1,0:T(8,128)(2,1)S(1)} collective-permute-done((bf16[520,128]{1,0:T(8,128)(2,1)S(1)}, bf16[520,128]{1,0:T(8,128)(2,1)S(1)}, u32[]{:S(2)}, u32[]{:S(2)}) %collective-permute-start.19) | collective-permute-done | bytes 133152 | tf_op jit(solution)/shard_map/ppermute | solution.py:36
  233.6 2.7 collective-permute-done.18
  236.3 1.9 collective-permute-done.17
  243.2 3.3 %collective-permute-done.22 = bf16[520,128]{1,0:T(8,128)(2,1)S(1)} collective-permute-done((bf16[520,128]{1,0:T(8,128)(2,1)}, bf16[520,128]{1,0:T(8,128)(2,1)S(1)}, u32[]{:S(2)}, u32[]{:S(2)}) %collective-permute-start.22) | collective-permute-done | bytes 133152 | tf_op jit(solution)/shard_map/ppermute | solution.py:36
  246.5 2.7 collective-permute-done.21
  255.1 2.9 %within.1 = (f32[512,768]{1,0:T(8,128)S(1)}, f32[8,768]{1,0:T(8,128)S(1)}) custom-call(bf16[512,768]{1,0:T(8,128)(2,1)S(1)} %copy-done.5, bf16[128,768]{1,0:T(8,128)(2,1)S(1)} %copy-done.9, bf16[128,768]{1,0:T(8,128)(2,1)S(1)} %copy-done.3, f32[8,768]{1,0:T(8,128)S(1)} %get-tuple-element.24.steps, f32[8,768]{1,0:T(8,128)S(1)} %get-tuple-element.25.logs, ...), custom_call_target="tpu_custom_call" | custom-call | flops 2000000000 | bytes 6000000 | tf_op jit(solution)/shard_map/within/pallas_call | solution.py:313
  258.0 8.2 %collective-permute-done.23 = bf16[520,128]{1,0:T(8,128)(2,1)S(1)} collective-permute-done((bf16[520,128]{1,0:T(8,128)(2,1)S(1)}, bf16[520,128]{1,0:T(8,128)(2,1)S(1)}, u32[]{:S(2)}, u32[]{:S(2)}) %collective-permute-start.23) | collective-permute-done | bytes 133152 | tf_op jit(solution)/shard_map/ppermute | solution.py:36
  266.3 1.7 finish.1
  (144 shorter events, 42.9 us)
Async XLA Ops:
  7.2 58.1 %copy-start = (bf16[4096,128]{1,0:T(8,128)(2,1)S(1)}, bf16[4096,128]{1,0:T(8,128)(2,1)}, u32[]{:S(2)}) copy-start(bf16[4096,128]{1,0:T(8,128)(2,1)} %param.26) | copy-start | bytes 3145732
  8.4 61.2 %collective-permute-start.3 = (bf16[1,144,640]{2,1,0:T(8,128)(2,1)S(1)}, bf16[1,144,640]{2,1,0:T(8,128)(2,1)S(1)}, u32[]{:S(2)}, u32[]{:S(2)}) collective-permute-start(bf16[1,144,640]{2,1,0:T(8,128)(2,1)S(1)} %fusion.24), channel_id=1, source_target_pairs={{0,6},{2,0},{4,2},{6,4},{1,7},{3,1},{5,3},{7,5},{8,14},{10,8},{12,... | collective-permute-start | bytes 552968 | tf_op jit(solution)/shard_map/ppermute | solution.py:36
  10.3 62.1 %collective-permute-start.2 = (bf16[1,144,640]{2,1,0:T(8,128)(2,1)S(1)}, bf16[1,144,640]{2,1,0:T(8,128)(2,1)S(1)}, u32[]{:S(2)}, u32[]{:S(2)}) collective-permute-start(bf16[1,144,640]{2,1,0:T(8,128)(2,1)S(1)} %fusion.24), channel_id=1, source_target_pairs={{0,4},{2,6},{4,0},{6,2},{1,5},{3,7},{5,1},{7,3},{8,12},{10,14},{12... | collective-permute-start | bytes 552968 | tf_op jit(solution)/shard_map/ppermute | solution.py:36
  11.8 60.6 %collective-permute-start.1 = (bf16[1,144,640]{2,1,0:T(8,128)(2,1)S(1)}, bf16[1,144,640]{2,1,0:T(8,128)(2,1)}, u32[]{:S(2)}, u32[]{:S(2)}) collective-permute-start(bf16[1,144,640]{2,1,0:T(8,128)(2,1)S(1)} %fusion.24), channel_id=1, source_target_pairs={{0,2},{2,4},{4,6},{6,0},{1,3},{3,5},{5,7},{7,1},{8,10},{10,12},{12... | collective-permute-start | bytes 552968 | tf_op jit(solution)/shard_map/ppermute | solution.py:36
  14.7 50.4 %copy-start.13 = (f32[4096]{0:T(1024)S(1)}, f32[4096]{0:T(1024)}, u32[]{:S(2)}) copy-start(f32[4096]{0:T(1024)} %param.23) | copy-start | bytes 49156
  14.7 62.6 %collective-permute-start.10 = (bf16[1,144,512]{2,1,0:T(8,128)(2,1)S(1)}, bf16[1,144,512]{2,1,0:T(8,128)(2,1)}, u32[]{:S(2)}, u32[]{:S(2)}) collective-permute-start(bf16[1,144,512]{2,1,0:T(8,128)(2,1)S(1)} %fusion.25), channel_id=1, source_target_pairs={{0,6},{2,0},{4,2},{6,4},{1,7},{3,1},{5,3},{7,5},{8,14},{10,8},{12,... | collective-permute-start | bytes 442376 | tf_op jit(solution)/shard_map/ppermute | solution.py:36
  14.8 62.5 %collective-permute-start.9 = (bf16[1,144,512]{2,1,0:T(8,128)(2,1)S(1)}, bf16[1,144,512]{2,1,0:T(8,128)(2,1)}, u32[]{:S(2)}, u32[]{:S(2)}) collective-permute-start(bf16[1,144,512]{2,1,0:T(8,128)(2,1)S(1)} %fusion.25), channel_id=1, source_target_pairs={{0,4},{2,6},{4,0},{6,2},{1,5},{3,7},{5,1},{7,3},{8,12},{10,14},{12... | collective-permute-start | bytes 442376 | tf_op jit(solution)/shard_map/ppermute | solution.py:36
  16.3 65.7 %all-to-all-start = ((bf16[12,144,256]{2,1,0:T(8,128)(2,1)}), bf16[12,144,256]{2,1,0:T(8,128)(2,1)}, u32[]{:S(2)}, u32[]{:S(2)}) async-start(bf16[12,144,256]{2,1,0:T(8,128)(2,1)} %bitcast.4), calls=%async_computation | async-start | bytes 1769472 | tf_op jit(solution)/shard_map/all_to_all | solution.py:395
  22.5 175.8 %all-gather.4.cloned.1.call-start = ((), (), s32[]{:S(2)}) async-start(), calls=%async_computation.3 | async-start | bytes 2193408 | tf_op jit(solution)/shard_map/all_gather | solution.py:413
  69.6 8.0 %collective-permute-start.8 = (bf16[1,144,512]{2,1,0:T(8,128)(2,1)S(1)}, bf16[1,144,512]{2,1,0:T(8,128)(2,1)S(1)}, u32[]{:S(2)}, u32[]{:S(2)}) collective-permute-start(bf16[1,144,512]{2,1,0:T(8,128)(2,1)S(1)} %fusion.25), channel_id=1, source_target_pairs={{0,2},{2,4},{4,6},{6,0},{1,3},{3,5},{5,7},{7,1},{8,10},{10,12},{12... | collective-permute-start | bytes 442376 | tf_op jit(solution)/shard_map/ppermute | solution.py:36
  73.4 19.8 %collective-permute-start.4 = (bf16[4,144,640]{2,1,0:T(8,128)(2,1)S(1)}, bf16[4,144,640]{2,1,0:T(8,128)(2,1)S(1)}, u32[]{:S(2)}, u32[]{:S(2)}) collective-permute-start(bf16[4,144,640]{2,1,0:T(8,128)(2,1)S(1)} %pad_maximum_fusion.1.rest_0_), channel_id=1, source_target_pairs={{0,8},{8,16},{16,24},{24,0},{1,9},{9,17},{17,25},{25,1},{2,10},{10... | collective-permute-start | bytes 2211848 | tf_op jit(solution)/shard_map/ppermute | solution.py:36
  75.0 18.6 %collective-permute-start.6 = (bf16[4,144,640]{2,1,0:T(8,128)(2,1)S(1)}, bf16[4,144,640]{2,1,0:T(8,128)(2,1)}, u32[]{:S(2)}, u32[]{:S(2)}) collective-permute-start(bf16[4,144,640]{2,1,0:T(8,128)(2,1)S(1)} %pad_maximum_fusion.1.rest_0_), channel_id=1, source_target_pairs={{0,24},{8,0},{16,8},{24,16},{1,25},{9,1},{17,9},{25,17},{2,26},{10... | collective-permute-start | bytes 2211848 | tf_op jit(solution)/shard_map/ppermute | solution.py:36
  78.6 19.3 %copy-start.14 = (f32[1152]{0:T(1024)S(1)}, f32[1152]{0:T(1024)}, u32[]{:S(2)}) copy-start(f32[1152]{0:T(1024)} %param.19) | copy-start | bytes 13828
  78.6 19.5 %collective-permute-start.11 = (bf16[4,144,512]{2,1,0:T(8,128)(2,1)S(1)}, bf16[4,144,512]{2,1,0:T(8,128)(2,1)}, u32[]{:S(2)}, u32[]{:S(2)}) collective-permute-start(bf16[4,144,512]{2,1,0:T(8,128)(2,1)S(1)} %pad_maximum_fusion.2.rest_5_), channel_id=1, source_target_pairs={{0,32},{32,64},{64,96},{96,0},{1,33},{33,65},{65,97},{97,1},{2,34}... | collective-permute-start | bytes 1769480 | tf_op jit(solution)/shard_map/ppermute | solution.py:36
  80.3 20.5 %collective-permute-start.13 = (bf16[4,144,512]{2,1,0:T(8,128)(2,1)S(1)}, bf16[4,144,512]{2,1,0:T(8,128)(2,1)}, u32[]{:S(2)}, u32[]{:S(2)}) collective-permute-start(bf16[4,144,512]{2,1,0:T(8,128)(2,1)S(1)} %pad_maximum_fusion.2.rest_5_), channel_id=1, source_target_pairs={{0,96},{32,0},{64,32},{96,64},{1,97},{33,1},{65,33},{97,65},{2,98}... | collective-permute-start | bytes 1769480 | tf_op jit(solution)/shard_map/ppermute | solution.py:36
  81.9 28.1 %collective-permute-start = (bf16[12,144,256]{2,1,0:T(8,128)(2,1)}, bf16[12,144,256]{2,1,0:T(8,128)(2,1)}, u32[]{:S(2)}, u32[]{:S(2)}) collective-permute-start(bf16[12,144,256]{2,1,0:T(8,128)(2,1)} %all-to-all-done), channel_id=1, source_target_pairs={{0,1},{1,0},{2,3},{3,2},{4,5},{5,4},{6,7},{7,6},{8,9},{9,8},{10,11... | collective-permute-start | bytes 2654216 | tf_op jit(solution)/shard_map/ppermute | solution.py:40
  93.2 16.8 %collective-permute-start.5 = (bf16[2,144,640]{2,1,0:T(8,128)(2,1)S(1)}, bf16[2,144,640]{2,1,0:T(8,128)(2,1)S(1)}, u32[]{:S(2)}, u32[]{:S(2)}) collective-permute-start(bf16[2,144,640]{2,1,0:T(8,128)(2,1)S(1)} %slice.120), channel_id=1, source_target_pairs={{0,8},{8,16},{16,24},{24,0},{1,9},{9,17},{17,25},{25,1},{2,10},{10... | collective-permute-start | bytes 1105928 | tf_op jit(solution)/shard_map/ppermute | solution.py:36
  94.6 15.4 %collective-permute-start.7 = (bf16[2,144,640]{2,1,0:T(8,128)(2,1)S(1)}, bf16[2,144,640]{2,1,0:T(8,128)(2,1)S(1)}, u32[]{:S(2)}, u32[]{:S(2)}) collective-permute-start(bf16[2,144,640]{2,1,0:T(8,128)(2,1)S(1)} %slice.121), channel_id=1, source_target_pairs={{0,24},{8,0},{16,8},{24,16},{1,25},{9,1},{17,9},{25,17},{2,26},{10... | collective-permute-start | bytes 1105928 | tf_op jit(solution)/shard_map/ppermute | solution.py:36
  99.1 10.4 %collective-permute-start.12 = (bf16[2,144,512]{2,1,0:T(8,128)(2,1)S(1)}, bf16[2,144,512]{2,1,0:T(8,128)(2,1)S(1)}, u32[]{:S(2)}, u32[]{:S(2)}) collective-permute-start(bf16[2,144,512]{2,1,0:T(8,128)(2,1)S(1)} %slice.122), channel_id=1, source_target_pairs={{0,32},{32,64},{64,96},{96,0},{1,33},{33,65},{65,97},{97,1},{2,34}... | collective-permute-start | bytes 884744 | tf_op jit(solution)/shard_map/ppermute | solution.py:36
  101.7 8.2 %collective-permute-start.14 = (bf16[2,144,512]{2,1,0:T(8,128)(2,1)S(1)}, bf16[2,144,512]{2,1,0:T(8,128)(2,1)S(1)}, u32[]{:S(2)}, u32[]{:S(2)}) collective-permute-start(bf16[2,144,512]{2,1,0:T(8,128)(2,1)S(1)} %slice.123), channel_id=1, source_target_pairs={{0,96},{32,0},{64,32},{96,64},{1,97},{33,1},{65,33},{97,65},{2,98}... | collective-permute-start | bytes 884744 | tf_op jit(solution)/shard_map/ppermute | solution.py:36
  128.7 1.9 collective-permute-start.15
  131.3 23.6 %copy-start.24 = (u32[256]{0:T(256)S(1)}, u32[256]{0:T(256)}, u32[]{:S(2)}) copy-start(u32[256]{0:T(256)} %constant.95) | copy-start | bytes 3076
  131.3 12.9 %all-to-all-start.1 = ((bf16[12,72,128]{2,1,0:T(8,128)(2,1)}), bf16[12,72,128]{2,1,0:T(8,128)(2,1)S(1)}, u32[]{:S(2)}, u32[]{:S(2)}) async-start(bf16[12,72,128]{2,1,0:T(8,128)(2,1)} %bitcast.9), calls=%async_computation.1 | async-start | bytes 442368 | tf_op jit(solution)/shard_map/all_to_all | solution.py:426
  145.7 34.8 %all-to-all-start.2 = ((bf16[32,72,128]{2,1,0:T(8,128)(2,1)}), bf16[32,72,128]{2,1,0:T(8,128)(2,1)S(1)}, u32[]{:S(2)}, u32[]{:S(2)}) async-start(bf16[32,72,128]{2,1,0:T(8,128)(2,1)} %bucket.1), calls=%async_computation.2 | async-start | bytes 1179648 | tf_op jit(solution)/shard_map/all_to_all | solution.py:429
  198.3 2.9 %collective-permute-start.16 = (bf16[4,144,768]{2,1,0:T(8,128)(2,1)}, bf16[4,144,768]{2,1,0:T(8,128)(2,1)}, u32[]{:S(2)}, u32[]{:S(2)}) collective-permute-start(bf16[4,144,768]{2,1,0:T(8,128)(2,1)} %bitcast.10.mine), channel_id=1, source_target_pairs={{0,1},{1,0},{2,3},{3,2},{4,5},{5,4},{6,7},{7,6},{8,9},{9,8},{10,11... | collective-permute-start | bytes 2654216 | tf_op jit(solution)/shard_map/ppermute | solution.py:40
  227.1 6.4 %collective-permute-start.19 = (bf16[520,128]{1,0:T(8,128)(2,1)S(1)}, bf16[520,128]{1,0:T(8,128)(2,1)S(1)}, u32[]{:S(2)}, u32[]{:S(2)}) collective-permute-start(bf16[520,128]{1,0:T(8,128)(2,1)S(1)} %convert_element_type.54), channel_id=1, source_target_pairs={{0,24},{8,0},{16,8},{24,16},{1,25},{9,1},{17,9},{25,17},{2,26},{10... | collective-permute-start | bytes 399368 | tf_op jit(solution)/shard_map/ppermute | solution.py:36
  228.4 7.9 %collective-permute-start.18 = (bf16[520,128]{1,0:T(8,128)(2,1)S(1)}, bf16[520,128]{1,0:T(8,128)(2,1)S(1)}, u32[]{:S(2)}, u32[]{:S(2)}) collective-permute-start(bf16[520,128]{1,0:T(8,128)(2,1)S(1)} %convert_element_type.54), channel_id=1, source_target_pairs={{0,16},{8,24},{16,0},{24,8},{1,17},{9,25},{17,1},{25,9},{2,18},{10... | collective-permute-start | bytes 399368 | tf_op jit(solution)/shard_map/ppermute | solution.py:36
  229.6 8.6 %collective-permute-start.17 = (bf16[520,128]{1,0:T(8,128)(2,1)S(1)}, bf16[520,128]{1,0:T(8,128)(2,1)S(1)}, u32[]{:S(2)}, u32[]{:S(2)}) collective-permute-start(bf16[520,128]{1,0:T(8,128)(2,1)S(1)} %convert_element_type.54), channel_id=1, source_target_pairs={{0,8},{8,16},{16,24},{24,0},{1,9},{9,17},{17,25},{25,1},{2,10},{10... | collective-permute-start | bytes 399368 | tf_op jit(solution)/shard_map/ppermute | solution.py:36
  239.9 6.6 %collective-permute-start.22 = (bf16[520,128]{1,0:T(8,128)(2,1)}, bf16[520,128]{1,0:T(8,128)(2,1)S(1)}, u32[]{:S(2)}, u32[]{:S(2)}) collective-permute-start(bf16[520,128]{1,0:T(8,128)(2,1)} %pad_maximum_fusion.3), channel_id=1, source_target_pairs={{0,96},{32,0},{64,32},{96,64},{1,97},{33,1},{65,33},{97,65},{2,98}... | collective-permute-start | bytes 399368 | tf_op jit(solution)/shard_map/ppermute | solution.py:36
  241.0 8.2 %collective-permute-start.21 = (bf16[520,128]{1,0:T(8,128)(2,1)}, bf16[520,128]{1,0:T(8,128)(2,1)S(1)}, u32[]{:S(2)}, u32[]{:S(2)}) collective-permute-start(bf16[520,128]{1,0:T(8,128)(2,1)} %pad_maximum_fusion.3), channel_id=1, source_target_pairs={{0,64},{32,96},{64,0},{96,32},{1,65},{33,97},{65,1},{97,33},{2,66}... | collective-permute-start | bytes 399368 | tf_op jit(solution)/shard_map/ppermute | solution.py:36
  242.6 8.3 %collective-permute-start.20 = (bf16[520,128]{1,0:T(8,128)(2,1)}, bf16[520,128]{1,0:T(8,128)(2,1)}, u32[]{:S(2)}, u32[]{:S(2)}) collective-permute-start(bf16[520,128]{1,0:T(8,128)(2,1)} %pad_maximum_fusion.3), channel_id=1, source_target_pairs={{0,32},{32,64},{64,96},{96,0},{1,33},{33,65},{65,97},{97,1},{2,34}... | collective-permute-start | bytes 399368 | tf_op jit(solution)/shard_map/ppermute | solution.py:36
  254.3 11.8 %collective-permute-start.23 = (bf16[520,128]{1,0:T(8,128)(2,1)S(1)}, bf16[520,128]{1,0:T(8,128)(2,1)S(1)}, u32[]{:S(2)}, u32[]{:S(2)}) collective-permute-start(bf16[520,128]{1,0:T(8,128)(2,1)S(1)} %pad_maximum_fusion.4), channel_id=1, source_target_pairs={{0,128},{128,0},{1,129},{129,1},{2,130},{130,2},{3,131},{131,3},{4... | collective-permute-start | bytes 399368 | tf_op jit(solution)/shard_map/ppermute | solution.py:36
  (21 other events, 152.7 us)
Sparse Core Ops, SparseCore 0:
  84.3 52.7 all-gather.3
